TPU v7x, 32 devices: a whole 2x2x4 slice. The times are simulated.
32 devices in a mesh: gz: 8 (over y, x, core), gy: 4 (over z).
Axes of the slice: x: 2, y: 2, z: 4, core: 2. Of those that a mesh axis runs over, the one named last changes fastest.
Arguments:
- orbitals: bfloat16 [256, 256, 512], P(('gz', 'gy')), may hold values from -2 to 2
- points: int32 [1024], replicated, may hold values from 0 to 131071, as said below
- coulomb: float32 [256, 512], P(None, 'gy'), may hold values from 10 to 1000
Outputs:
- potentials: bfloat16 [256, 512, 1024], P('gz', 'gy')
Inputs may be any that keep to these rules, and one draw needn't show every extreme that they name: `points`: 1024 distinct grid cells.
All inputs are finite; a program needn't handle non-finite values.
Results may differ from a plain program's by a relative error of at most 0.0025.
Values may be sent and summed in bfloat16 or wider, within the bound.
No kernel may reach another device: no remote copies, remote signals or barrier semaphores. Data moves between devices by JAX's collectives and lax.ppermute only.
A program may use at most 192 MiB of HBM per device.

v0:
```python
import math

import jax
import jax.numpy as jnp
from jax import lax
from jax.sharding import PartitionSpec as P


def transform(values_in, kernel):
    planes, col_width, item_count = values_in.shape
    positions = jnp.arange(planes, dtype=jnp.int32)
    angles = (
        2.0
        * math.pi
        / planes
        * (positions[:, None] * positions[None, :] % planes).astype(jnp.float32)
    )
    cosine = jnp.cos(angles)
    sine_table = jnp.sin(angles)
    stacked = values_in.reshape(planes, col_width * item_count)
    real_part = jnp.dot(
        cosine, stacked, precision=lax.Precision.HIGHEST, preferred_element_type=jnp.float32
    )
    imag_part = jnp.dot(
        sine_table, stacked, precision=lax.Precision.HIGHEST, preferred_element_type=jnp.float32
    )
    real_part = (real_part.reshape(planes, col_width, item_count) * kernel[:, :, None]).reshape(
        planes, -1
    )
    imag_part = (imag_part.reshape(planes, col_width, item_count) * kernel[:, :, None]).reshape(
        planes, -1
    )
    back = jnp.dot(
        cosine, real_part, precision=lax.Precision.HIGHEST, preferred_element_type=jnp.float32
    )
    back = back + jnp.dot(
        sine_table, imag_part, precision=lax.Precision.HIGHEST, preferred_element_type=jnp.float32
    )
    return (back / planes).reshape(planes, col_width, item_count)


def per_device(orbitals, points, coulomb):
    gz_count = lax.axis_size("gz")
    gy_count = lax.axis_size("gy")
    bands_local, planes, columns = orbitals.shape
    col_block = columns // gy_count
    col_pencil = col_block // gz_count
    slab_planes = planes // gz_count
    point_count = points.shape[0]
    total_bands = bands_local * gz_count * gy_count
    regrouped = lax.all_to_all(
        lax.all_to_all(orbitals, "gz", split_axis=1, concat_axis=0, tiled=True),
        "gy",
        split_axis=2,
        concat_axis=0,
        tiled=True,
    )
    plane_start = lax.axis_index("gz") * slab_planes
    col_start = lax.axis_index("gy") * col_block
    plane_ids = plane_start + jnp.arange(slab_planes, dtype=jnp.int32)
    column_ids = col_start + jnp.arange(col_block, dtype=jnp.int32)
    cell_ids = (plane_ids[:, None] * columns + column_ids[None, :]).reshape(-1)
    flattened = regrouped.reshape(total_bands, -1)
    selector = (cell_ids[:, None] == points[None, :]).astype(jnp.bfloat16)
    partial_rows = jnp.dot(flattened, selector, preferred_element_type=jnp.float32)
    at_points = lax.psum(partial_rows, ("gz", "gy")).astype(jnp.bfloat16)
    pair_base = lax.dot_general(
        at_points, at_points, (((0,), (0,)), ((), ())), preferred_element_type=jnp.float32
    )
    pair_gram = pair_base * pair_base
    factor = jnp.linalg.cholesky(pair_gram)
    inverse = jax.scipy.linalg.cho_solve((factor, True), jnp.eye(point_count, dtype=jnp.float32))
    sums = lax.dot_general(
        flattened, at_points, (((0,), (0,)), ((), ())), preferred_element_type=jnp.float32
    )
    fitted = jnp.dot(
        sums * sums, inverse, precision=lax.Precision.HIGHEST, preferred_element_type=jnp.float32
    )
    kernel = lax.dynamic_slice_in_dim(coulomb, lax.axis_index("gz") * col_pencil, col_pencil, 1)
    slab_fields = fitted.reshape(slab_planes, col_block, point_count)
    potential = transform(
        lax.all_to_all(slab_fields, "gz", split_axis=1, concat_axis=0, tiled=True), kernel
    ).astype(jnp.bfloat16)
    return lax.all_to_all(potential, "gz", split_axis=0, concat_axis=1, tiled=True)


def solution(mesh):
    return jax.shard_map(
        per_device,
        mesh=mesh,
        in_specs=(P(("gz", "gy"), None, None), P(), P(None, "gy")),
        out_specs=P("gz", "gy", None),
        check_vma=False,
    )
```

profile of v0, /device:TPU:1, one launch (start us, length us, event | category | flops | bytes accessed | tf_op | source)
XLA Modules:
  0.0 1122.5 jit_solution(6071485466699631778)
XLA Ops:
  0.0 2.8 copy.46
  2.8 30.3 %all_to_all.66 = bf16[8,256,512]{2,0,1:T(8,128)(2,1)S(1)} all-to-all(bf16[8,256,512]{2,0,1:T(8,128)(2,1)S(1)} %copy.46), channel_id=1, replica_groups=mesh['gz'=8,'gy'=4] {'gz'}, dimensions={1} | all-to-all | bytes 4194304 | tf_op jit(solution)/shard_map/all_to_all | solution.py:52
  33.9 7.8 copy.49
  41.7 5.9 reshape.178
  47.6 4.6 all-to-all-start.1
  56.1 43.8 %all-to-all-done.1 = bf16[4,2,131072]{2,1,0:T(2,128)(2,1)S(1)} async-done(((bf16[4,2,131072]{2,1,0:T(2,128)(2,1)}), bf16[4,2,131072]{2,1,0:T(2,128)(2,1)S(1)}, u32[]{:S(2)}, u32[]{:S(2)}) %all-to-all-start.1) | async-done | bytes 2097184 | tf_op jit(solution)/shard_map/all_to_all | solution.py:51
  99.9 4.0 reshape.179
  103.8 7.7 copy.50
  111.6 4.1 fusion.41
  115.7 46.7 %all-reduce.2 = bf16[256,1024]{0,1:T(8,128)(2,1)S(1)} all-reduce(f32[256,1024]{0,1:T(8,128)} %fusion.41), channel_id=1, replica_groups=mesh['gz'=8,'gy'=4] {'gz','gy'}, use_global_device_ids=true, to_apply=%region_0.0 | all-reduce | flops 262144 | bytes 1572864 | tf_op jit(solution)/shard_map/psum | solution.py:66
  162.4 2.8 convolution_multiply_fusion.2
  165.1 8.1 fusion.8
  173.3 5.3 copy.53
  178.6 4.4 fusion.7
  185.0 11.7 %cholesky.223 = f32[128,128]{1,0:T(8,128)S(1)} custom-call(f32[128,128]{1,0:T(8,128)S(1)} %cholesky.580), custom_call_target="Cholesky" | custom-call | tf_op jit(solution)/shard_map/jit(cholesky)/cholesky | solution.py:71
  196.8 9.8 custom-call.66
  213.0 20.4 %cholesky.244 = f32[128,128]{1,0:T(8,128)S(1)} custom-call(f32[128,128]{1,0:T(8,128)S(1)} %cholesky.584), custom_call_target="Cholesky" | custom-call | tf_op jit(solution)/shard_map/jit(cholesky)/cholesky | solution.py:71
  234.0 9.8 custom-call.67
  247.1 11.7 %cholesky.468 = f32[128,128]{1,0:T(8,128)S(1)} custom-call(f32[128,128]{1,0:T(8,128)S(1)} %cholesky.589), custom_call_target="Cholesky" | custom-call | tf_op jit(solution)/shard_map/jit(cholesky)/cholesky | solution.py:71
  260.2 9.8 custom-call.68
  273.5 11.9 %cholesky.487 = f32[128,128]{1,0:T(8,128)S(1)} custom-call(f32[128,128]{1,0:T(8,128)S(1)} %cholesky.594), custom_call_target="Cholesky" | custom-call | tf_op jit(solution)/shard_map/jit(cholesky)/cholesky | solution.py:71
  286.7 9.8 custom-call.69
  300.0 11.7 %cholesky.506 = f32[128,128]{1,0:T(8,128)S(1)} custom-call(f32[128,128]{1,0:T(8,128)S(1)} %cholesky.599), custom_call_target="Cholesky" | custom-call | tf_op jit(solution)/shard_map/jit(cholesky)/cholesky | solution.py:71
  313.0 10.2 custom-call.70
  326.5 11.7 %cholesky.526 = f32[128,128]{1,0:T(8,128)S(1)} custom-call(f32[128,128]{1,0:T(8,128)S(1)} %cholesky.604), custom_call_target="Cholesky" | custom-call | tf_op jit(solution)/shard_map/jit(cholesky)/cholesky | solution.py:71
  339.5 9.8 custom-call.71
  352.3 11.9 %cholesky.546 = f32[128,128]{1,0:T(8,128)S(1)} custom-call(f32[128,128]{1,0:T(8,128)S(1)} %cholesky.609), custom_call_target="Cholesky" | custom-call | tf_op jit(solution)/shard_map/jit(cholesky)/cholesky | solution.py:71
  365.5 9.8 custom-call.72
  377.9 11.7 %cholesky.564 = f32[128,128]{1,0:T(8,128)S(1)} custom-call(f32[128,128]{1,0:T(8,128)S(1)} %convolution_subtract_fusion.16), custom_call_target="Cholesky" | custom-call | tf_op jit(solution)/shard_map/jit(cholesky)/cholesky | solution.py:71
  396.6 4.9 select_select_fusion
  401.5 22.9 %while.1 = (s32[]{:T(128)}, f32[1024,1024]{1,0:T(8,128)}, s32[8,2]{0,1:T(2,128)S(1)}, f32[8,128,128]{2,1,0:T(8,128)S(1)}, s32[]{:T(128)}) while((s32[]{:T(128)}, f32[1024,1024]{1,0:T(8,128)}, s32[8,2]{0,1:T(2,128)S(1)}, f32[8,128,128]{2,1,0:T(8,128)S(1)}, s32[]{:T(128)}) %tuple.56), condition=%wide.while_cond, body=%wide.while_body.sunk | while | flops 2 | bytes 131189 | solution.py:72
  424.4 79.0 %custom-call.73 = f32[8,128,128]{1,2,0:T(8,128)S(1)} custom-call(f32[8,128,128]{2,1,0:T(8,128)S(1)} %get-tuple-element.12), custom_call_target="InvertDiagBlocksLowerTriangular" | custom-call | tf_op jit(solution)/shard_map/jit(_cho_solve)/triangular_solve | solution.py:72
  538.7 56.2 %fusion.2 = f32[4096,1024]{1,0:T(8,128)} fusion(f32[1024,1024]{1,0:T(8,128)S(1)} %constant_dynamic-update-slice_fusion.36, f32[1024,4096]{1,0:T(8,128)S(1)} %bitcast.191), kind=kOutput, calls=%fused_computation.5 | convolution fusion | flops 51543801856 | bytes 37748736 | tf_op jit(solution)/shard_map/dot_general | solution.py:76
  594.8 17.7 %copy.54 = f32[32,128,1024]{2,0,1:T(8,128)} copy(f32[32,128,1024]{2,1,0:T(8,128)} %bitcast.194) | data formatting | bytes 33554432 | tf_op jit(solution)/shard_map/reshape | solution.py:80
  612.6 7.8 all-to-all-start.2
  620.6 180.3 %all-to-all-done.2 = f32[32,128,1024]{2,0,1:T(8,128)} async-done(((f32[32,128,1024]{2,0,1:T(8,128)}), f32[32,128,1024]{2,0,1:T(8,128)}, u32[]{:S(2)}, u32[]{:S(2)}) %all-to-all-start.2) | async-done | bytes 16777248 | tf_op jit(solution)/shard_map/all_to_all | solution.py:82
  800.8 15.2 %copy.56 = f32[8,32,16,1024]{3,2,1,0:T(8,128)S(1)} copy(f32[8,32,16,1024]{3,1,2,0:T(8,128)} %bitcast.35) | data formatting | bytes 33554432 | tf_op jit(solution)/shard_map/all_to_all | solution.py:82
  816.1 13.8 %copy.66 = f32[32,8,16,1024]{3,1,2,0:T(8,128)} copy(f32[32,8,16,1024]{3,2,1,0:T(8,128)S(1)} %bitcast.184) | data formatting | bytes 33554432
  829.8 17.5 %copy.57 = f32[16384,256]{1,0:T(8,128)} copy(f32[16384,256]{0,1:T(8,128)} %bitcast.185) | data formatting | bytes 33554432 | tf_op jit(solution)/shard_map/dot_general | solution.py:21
  847.3 23.6 %convolution_multiply_fusion = f32[256,16,1024]{2,0,1:T(8,128)} fusion(f32[16,1024,256]{2,1,0:T(8,128)} %bitcast.181, f32[256,16]{0,1:T(8,128)S(1)} %copy.58), kind=kOutput, calls=%fused_computation.8 | convolution fusion | flops 12890013696 | bytes 33570816 | tf_op jit(solution)/shard_map/dot_general | solution.py:24
  870.8 23.7 %convolution_multiply_fusion.1 = f32[256,16,1024]{2,0,1:T(8,128)} fusion(f32[16,1024,256]{2,1,0:T(8,128)} %bitcast.182, f32[256,16]{0,1:T(8,128)S(1)} %copy.58), kind=kOutput, calls=%fused_computation.9 | convolution fusion | flops 12890013696 | bytes 33570816 | tf_op jit(solution)/shard_map/dot_general | solution.py:21
  894.6 17.6 %copy.59 = f32[256,16,1024]{0,2,1:T(8,128)} copy(f32[256,16,1024]{2,0,1:T(8,128)} %convolution_multiply_fusion.1) | data formatting | bytes 33554432 | tf_op jit(solution)/shard_map/mul | solution.py:27
  912.2 23.4 %fusion.107 = f32[256,16384]{1,0:T(8,128)} fusion(f32[256,16384]{0,1:T(8,128)} %bitcast.186), kind=kOutput, calls=%fused_computation.135 | convolution fusion | flops 12885819392 | bytes 33554432 | tf_op jit(solution)/shard_map/dot_general | solution.py:33
  935.6 17.6 %copy.60 = f32[256,16,1024]{0,2,1:T(8,128)} copy(f32[256,16,1024]{2,0,1:T(8,128)} %convolution_multiply_fusion) | data formatting | bytes 33554432 | tf_op jit(solution)/shard_map/mul | solution.py:30
  953.1 42.9 %fusion.1 = bf16[256,16384]{1,0:T(8,128)(2,1)} fusion(f32[256,16384]{1,0:T(8,128)} %fusion.107, f32[256,16384]{0,1:T(8,128)} %bitcast.183), kind=kOutput, calls=%fused_computation.4 | convolution fusion | flops 12898402304 | bytes 41943040 | tf_op jit(solution)/shard_map/dot_general | solution.py:36
  996.1 15.2 %copy.67 = bf16[32,8,16,1024]{3,2,1,0:T(8,128)(2,1)} copy(bf16[32,8,16,1024]{3,1,2,0:T(8,128)(2,1)} %bitcast.187) | data formatting | bytes 16777216
  1011.3 102.1 %all_to_all.67 = bf16[256,16,1024]{2,1,0:T(8,128)(2,1)} all-to-all(bf16[256,16,1024]{2,1,0:T(8,128)(2,1)} %bitcast.188), channel_id=1, replica_groups=mesh['gz'=8,'gy'=4] {'gz'}, dimensions={0} | all-to-all | bytes 16777216 | tf_op jit(solution)/shard_map/all_to_all | solution.py:84
  1113.4 8.7 copy.61
  (145 shorter events, 99.0 us)
Async XLA Ops:
  0.0 620.4 %copy-start = (f32[256,128]{1,0:T(8,128)S(1)}, f32[256,128]{1,0:T(8,128)}, u32[]{:S(2)}) copy-start(f32[256,128]{1,0:T(8,128)} %param.5) | copy-start | bytes 393220
  47.6 52.3 %all-to-all-start.1 = ((bf16[4,2,131072]{2,1,0:T(2,128)(2,1)}), bf16[4,2,131072]{2,1,0:T(2,128)(2,1)S(1)}, u32[]{:S(2)}, u32[]{:S(2)}) async-start(bf16[4,2,131072]{2,1,0:T(2,128)(2,1)} %reshape.178), calls=%async_computation.1 | async-start | bytes 4194304 | tf_op jit(solution)/shard_map/all_to_all | solution.py:51
  103.8 7.8 copy-start.5
  183.0 2.0 copy-start.4
  503.4 3.9 copy-start.2
  506.5 3.6 copy-start.3
  531.2 6.2 slice-start
  531.4 6.0 slice-start.1
  534.1 3.3 slice-start.2
  536.5 2.2 slice-start.3
  612.6 188.3 %all-to-all-start.2 = ((f32[32,128,1024]{2,0,1:T(8,128)}), f32[32,128,1024]{2,0,1:T(8,128)}, u32[]{:S(2)}, u32[]{:S(2)}) async-start(f32[32,128,1024]{2,0,1:T(8,128)} %copy.54), calls=%async_computation.2 | async-start | bytes 33554432 | tf_op jit(solution)/shard_map/all_to_all | solution.py:82
  1113.4 8.7 copy-start.1
where the time goes:
time: 1130 us; the launch traced here: 1120 us
  other arithmetic  273 us (24%)
  matrix products  240 us (21%)
  waiting for transfers between devices  224 us (20%)
  local copies, waits for them, and re-layouts  187 us (17%)
  blocking collectives  179 us (16%)
  starting transfers between devices  12.4 us (1%)
    another operation x30, other arithmetic, per_device(): factor = jnp.linalg.cholesky(pair_gram)  181 us
    all_to_all x1, waiting for transfers between devices, per_device(): lax.all_to_all(slab_fields, 'gz', split_axis=1, concat_axis=0, tiled=True)  180 us
    all_to_all x1, blocking collectives, per_device(): lax.all_to_all(potential, 'gz', split_axis=0, concat_axis=1, tiled=True)  102 us
    another operation x3, other arithmetic, per_device(): jax.scipy.linalg.cho_solve((factor, True), jnp.eye(point_count, dtype=jnp...  83.9 us
    dot_general x1, matrix products, per_device(): jnp.dot(sums * sums, inverse, precision=lax.Precision.HIGHEST, preferred_...  56.2 us
    psum x1, blocking collectives, per_device(): at_points = lax.psum(partial_rows, ('gz', 'gy')).astype(jnp.bfloat16)  46.7 us
    unnamed x43, local copies, waits for them, and re-layouts  45.6 us
    all_to_all x1, waiting for transfers between devices, per_device(): lax.all_to_all(lax.all_to_all(orbitals, 'gz', split_axis=1, concat_axis=0...  43.8 us
  transfers between devices with their start and end apart: 2, of which 2 were waited for; matrix products, arithmetic and copies ran while one was open for 0% of the time, Pallas kernels for 0%

commit v1 on v0

v1 whole, which is shorter than its diff:
```python
import functools
import math

import jax
import jax.numpy as jnp
import numpy as np
from jax import lax
from jax.experimental import pallas as pl
from jax.experimental.pallas import tpu as pltpu
from jax.sharding import PartitionSpec as P

F32 = jnp.float32
BF16 = jnp.bfloat16
HIGH = lax.Precision.HIGHEST
MIB = 1024 * 1024


def split(value):
    high = value.astype(BF16)
    return high, (value - high.astype(F32)).astype(BF16)


def points_kernel(points_ref, field_ref, out_ref, *, columns):
    bands = field_ref.shape[1]
    lane = lax.broadcasted_iota(jnp.int32, (bands, 128), 1)

    def tile(t, _):
        base = pl.multiple_of(t * 128, 128)

        def some(s, acc):
            for u in range(16):
                m = s * 16 + u
                cell = points_ref[base + m]
                plane = cell // columns
                column = cell - plane * columns
                at = pl.multiple_of(plane // 128 * 128, 128)
                row = field_ref[column, :, pl.ds(at, 128)]
                row = pltpu.roll(row, (m - plane + at + 128) % 128, 1)
                acc = jnp.where(lane == m, row, acc)
            return acc

        acc = lax.fori_loop(0, 8, some, jnp.zeros((bands, 128), F32))
        out_ref[:, pl.ds(base, 128)] = acc
        return 0

    lax.fori_loop(0, points_ref.shape[0] // 128, tile, 0)


def take_points(points, field, columns):
    return pl.pallas_call(
        functools.partial(points_kernel, columns=columns),
        out_shape=jax.ShapeDtypeStruct((field.shape[1], points.shape[0]), F32),
        in_specs=[
            pl.BlockSpec(memory_space=pltpu.SMEM),
            pl.BlockSpec(memory_space=pltpu.VMEM),
        ],
        out_specs=pl.BlockSpec(memory_space=pltpu.VMEM),
        compiler_params=pltpu.CompilerParams(vmem_limit_bytes=32 * MIB),
        name="take_points",
    )(points, field)


def sweep_small(a):
    n = a.shape[0]
    lane = lax.broadcasted_iota(jnp.int32, (8, n), 1)
    wide = lax.broadcasted_iota(jnp.int32, (n, n), 1)
    sub = lax.broadcasted_iota(jnp.int32, (8, n), 0)
    for g in range(n // 8):
        lo = 8 * g
        rows = a[lo : lo + 8, :]
        cols = [jnp.broadcast_to(a[:, lo + j : lo + j + 1], (n, n)) for j in range(8)]
        t = [c[lo : lo + 8, :] for c in cols]
        for k in range(8):
            pivot = jnp.broadcast_to(t[k][k : k + 1, :], (8, n))
            scale = 1.0 / pivot
            here = sub == k
            new = []
            for j in range(8):
                if j == k:
                    new.append(jnp.where(here, -scale, t[k] * scale))
                else:
                    factor = jnp.broadcast_to(t[j][k : k + 1, :], (8, n)) * scale
                    new.append(jnp.where(here, factor, t[j] - t[k] * factor))
            t = new
        q = None
        for j in range(8):
            term = t[j] * jnp.broadcast_to(rows[j : j + 1, :], (8, n))
            q = term if q is None else q + term
        q = -q
        for j in range(8):
            q = jnp.where(lane == lo + j, t[j], q)
        inside = (wide >= lo) & (wide < lo + 8)
        upd = jnp.where(inside, 0.0, a)
        for j in range(8):
            upd = upd - cols[j] * jnp.broadcast_to(q[j : j + 1, :], (n, n))
        a = jnp.concatenate(
            ([upd[:lo]] if lo else []) + [q] + ([upd[lo + 8 :]] if lo + 8 < n else []), axis=0
        )
    return a


def mm(a, b):
    return jnp.dot(a, b, precision=HIGH, preferred_element_type=F32)


def inverse_kernel(values_ref, high_ref, low_ref, gram, block, panel, *, big, small):
    n = gram.shape[0]

    @pl.loop(0, n // big)
    def _(t):
        r = pl.ds(pl.multiple_of(t * big, big), big)
        base = lax.dot_general(
            values_ref[:, r], values_ref[...], (((0,), (0,)), ((), ())), preferred_element_type=F32
        )
        gram[r, :] = base * base

    inner = lax.broadcasted_iota(jnp.int32, (small, big), 1)
    inner_full = lax.broadcasted_iota(jnp.int32, (big, big), 1)

    @pl.loop(0, n // big)
    def _(k):
        at = pl.multiple_of(k * big, big)
        kr = pl.ds(at, big)
        block[...] = gram[kr, kr]
        for s in range(big // small):
            lo = s * small
            sr = slice(lo, lo + small)
            negative = sweep_small(block[sr, sr])
            q = -mm(negative, block[sr, :])
            inside = (inner >= lo) & (inner < lo + small)
            q = jnp.where(inside, jnp.concatenate([negative] * (big // small), axis=1), q)
            inside_full = (inner_full >= lo) & (inner_full < lo + small)
            upd = jnp.where(inside_full, 0.0, block[...]) - mm(block[:, sr], q)
            block[...] = upd
            block[sr, :] = q
        panel[...] = -mm(block[...], gram[kr, :])
        panel[:, kr] = block[...]
        wide = lax.broadcasted_iota(jnp.int32, (big, n), 1)
        inside = (wide >= at) & (wide < at + big)

        @pl.loop(0, n // big)
        def _(t):
            r = pl.ds(pl.multiple_of(t * big, big), big)
            col = gram[r, kr]
            gram[r, :] = jnp.where(inside, 0.0, gram[r, :]) - mm(col, panel[...])

        gram[kr, :] = panel[...]

    @pl.loop(0, n // big)
    def _(t):
        r = pl.ds(pl.multiple_of(t * big, big), big)
        high, low = split(-gram[r, :])
        high_ref[r, :] = high
        low_ref[r, :] = low


def invert_gram(values):
    bands, n = values.shape
    big, small = 256, 128
    shape = jax.ShapeDtypeStruct((n, n), BF16)
    return pl.pallas_call(
        functools.partial(inverse_kernel, big=big, small=small),
        out_shape=(shape, shape),
        in_specs=[pl.BlockSpec(memory_space=pltpu.VMEM)],
        out_specs=(pl.BlockSpec(memory_space=pltpu.VMEM),) * 2,
        scratch_shapes=[
            pltpu.VMEM((n, n), F32),
            pltpu.VMEM((big, big), F32),
            pltpu.VMEM((big, n), F32),
        ],
        compiler_params=pltpu.CompilerParams(vmem_limit_bytes=40 * MIB),
        cost_estimate=pl.CostEstimate(
            flops=12 * n**3, bytes_accessed=6 * n * n, transcendentals=0
        ),
        name="invert_gram",
    )(values)


def column_kernel(fields_ref, values_ref, circ_ref, high_ref, low_ref):
    planes_out = high_ref.shape[1]
    for i in range(high_ref.shape[0]):
        field = fields_ref[:, i].reshape(values_ref.shape[0], fields_ref.shape[-1])
        sums = lax.dot_general(
            field, values_ref[...], (((0,), (0,)), ((), ())), preferred_element_type=F32
        )
        high, low = split(sums * sums)
        both = jnp.dot(circ_ref[i], high, preferred_element_type=F32)
        both = both + jnp.dot(circ_ref[i], low, preferred_element_type=F32)
        w_high, w_low = split(both[:planes_out] + both[planes_out:])
        high_ref[i] = w_high
        low_ref[i] = w_low


def convolve(fields, values, circ):
    quads, cols, rows, planes = fields.shape
    bands, n = values.shape
    out_planes = circ.shape[1] // 2
    step = 2
    shape = jax.ShapeDtypeStruct((cols, out_planes, n), BF16)
    out_spec = pl.BlockSpec((step, out_planes, n), lambda j: (j, 0, 0))
    return pl.pallas_call(
        column_kernel,
        grid=(cols // step,),
        out_shape=(shape, shape),
        in_specs=[
            pl.BlockSpec((quads, step, rows, planes), lambda j: (0, j, 0, 0)),
            pl.BlockSpec((bands, n), lambda j: (0, 0)),
            pl.BlockSpec((step, 2 * out_planes, planes), lambda j: (j, 0, 0)),
        ],
        out_specs=(out_spec, out_spec),
        compiler_params=pltpu.CompilerParams(vmem_limit_bytes=40 * MIB),
        cost_estimate=pl.CostEstimate(
            flops=2 * cols * n * planes * (bands + 4 * out_planes),
            bytes_accessed=2 * (quads * cols * rows * planes + 2 * cols * out_planes * n),
            transcendentals=0,
        ),
        name="convolve",
    )(fields, values, circ)


def fit_kernel(w_high_ref, w_low_ref, high_ref, low_ref, out_ref):
    w_high = w_high_ref[...]
    acc = jnp.dot(w_high, high_ref[...], preferred_element_type=F32)
    acc = acc + jnp.dot(w_high, low_ref[...], preferred_element_type=F32)
    acc = acc + jnp.dot(w_low_ref[...], high_ref[...], preferred_element_type=F32)
    out_ref[...] = acc.astype(out_ref.dtype)


def fit(w_high, w_low, high, low):
    rows, n = w_high.shape
    step = 512
    row_spec = pl.BlockSpec((step, n), lambda i: (i, 0))
    full_spec = pl.BlockSpec((n, n), lambda i: (0, 0))
    return pl.pallas_call(
        fit_kernel,
        grid=(rows // step,),
        out_shape=jax.ShapeDtypeStruct((rows, n), BF16),
        in_specs=[row_spec, row_spec, full_spec, full_spec],
        out_specs=row_spec,
        compiler_params=pltpu.CompilerParams(vmem_limit_bytes=48 * MIB),
        cost_estimate=pl.CostEstimate(
            flops=6 * rows * n * n, bytes_accessed=6 * rows * n + 4 * n * n, transcendentals=0
        ),
        name="fit",
    )(w_high, w_low, high, low)


def per_device(orbitals, points, coulomb):
    gz_count = lax.axis_size("gz")
    gy_count = lax.axis_size("gy")
    gz = lax.axis_index("gz")
    gy = lax.axis_index("gy")
    bands_local, planes, columns = orbitals.shape
    col_block = columns // gy_count
    half = col_block // 2
    slab = planes // gz_count
    pairs = gz_count // 2
    me = gz % 2
    pair = gz // 2

    turned = jnp.transpose(orbitals, (2, 0, 1))
    local_values = take_points(points, turned.astype(F32), columns).astype(BF16)
    gathered = lax.all_gather(local_values, ("gz", "gy"), axis=0, tiled=True)

    blocks = turned.reshape(gy_count, 2, half, bands_local, planes)
    slots = []
    for dg in range(gy_count):
        for dc in range(2):
            part = lax.dynamic_slice(
                blocks,
                ((gy + dg) % gy_count, me ^ dc, 0, 0, 0),
                (1, 1, half, bands_local, planes),
            )[0, 0]
            if dg or dc:
                perm = [
                    (z * gy_count + y, (z ^ dc) * gy_count + (y + dg) % gy_count)
                    for z in range(gz_count)
                    for y in range(gy_count)
                ]
                part = lax.ppermute(part, ("gz", "gy"), perm)
            slots.append(part)
    mine = jnp.concatenate(slots, axis=1)
    groups = [[2 * p + c for p in range(pairs)] for c in range(2)]
    fields = lax.all_gather(mine, "gz", axis=0, axis_index_groups=groups)

    slot_ids = jnp.arange(gy_count * 2, dtype=jnp.int32)
    from_gy = (gy - slot_ids // 2) % gy_count
    from_me = me ^ (slot_ids % 2)
    source = (2 * jnp.arange(pairs, dtype=jnp.int32)[:, None] + from_me[None, :]) * gy_count
    source = (source + from_gy[None, :]).reshape(-1)
    ordered = jnp.take(
        gathered.reshape(-1, bands_local, points.shape[0]), source, axis=0
    ).reshape(gathered.shape)

    high, low = invert_gram(gathered)

    grid = np.arange(planes, dtype=np.int64)
    angles = (2.0 * np.pi / planes) * ((grid[:, None] * grid[None, :]) % planes)
    table = np.concatenate([np.cos(angles), np.sin(angles)], axis=1)
    out_rows = lax.dynamic_slice_in_dim(
        jnp.asarray(table, F32), pair * (2 * slab), 2 * slab, 0
    )
    kernel = lax.dynamic_slice_in_dim(coulomb, me * half, half, 1).T
    kernel = jnp.concatenate([kernel, kernel], axis=1)
    weighted = (kernel[:, None, :] * out_rows[None]).reshape(half * 2 * slab, 2 * planes)
    circ = jnp.dot(
        weighted, jnp.asarray(table.T / planes, F32), precision=HIGH, preferred_element_type=F32
    ).reshape(half, 2 * slab, planes)
    coarse = lax.reduce_precision(circ, 8, 7)
    circ = jnp.concatenate([coarse, circ - coarse], axis=1).astype(BF16)

    w_high, w_low = convolve(fields, ordered, circ)
    n = points.shape[0]
    result = fit(w_high.reshape(-1, n), w_low.reshape(-1, n), high, low)
    result = result.reshape(half, 2, slab, n)
    own = lax.dynamic_index_in_dim(result, me, 1, keepdims=False)
    other = lax.dynamic_index_in_dim(result, 1 - me, 1, keepdims=False)
    other = lax.ppermute(other, "gz", [(z, z ^ 1) for z in range(gz_count)])
    first = jnp.where(me == 0, own, other)
    second = jnp.where(me == 0, other, own)
    return jnp.transpose(jnp.concatenate([first, second], axis=0), (1, 0, 2))


def solution(mesh):
    return jax.shard_map(
        per_device,
        mesh=mesh,
        in_specs=(P(("gz", "gy"), None, None), P(), P(None, "gy")),
        out_specs=P("gz", "gy", None),
        check_vma=False,
    )
```

time: 1130 us -> 349 us (0.31)
  other arithmetic: 273 us -> 22.6 us
  matrix products: 240 us -> 6.95 us
  waiting for transfers between devices: 224 us -> 31.8 us
  local copies, waits for them, and re-layouts: 187 us -> 29.7 us
  Pallas kernels: 0 us -> 148 us
  blocking collectives: 179 us -> 77.7 us
    another operation x33 -> x0, other arithmetic: 265 us -> none  [the longest x30 181 us: per_device(): factor = jnp.linalg.cholesky(pair_gram)]
    all_to_all x2 -> x0, waiting for transfers between devices: 224 us -> none  [the longest x1 180 us: per_device(): lax.all_to_all(slab_fields, 'gz', split_axis=1, concat_axis=0, tiled=True)]
    dot_general x8 -> x1, matrix products: 185 us -> 6.95 us  [per_device(): jnp.dot(weighted, jnp.asarray(table.T / planes, F32), precision=HIGH, pre...]
    pallas_call x0 -> x4, Pallas kernels: none -> 148 us  [the longest x1 64.7 us: invert_gram(): pl.pallas_call(functools.partial(inverse_kernel, big=big, small=small), o...]
    all_to_all x2 -> x0, blocking collectives: 132 us -> none  [the longest x1 102 us: per_device(): lax.all_to_all(potential, 'gz', split_axis=0, concat_axis=1, tiled=True)]
    all_gather x0 -> x1, blocking collectives: none -> 77.7 us  [per_device(): gathered = lax.all_gather(local_values, ('gz', 'gy'), axis=0, tiled=True)]
    another operation x44 -> x0, matrix products: 55.5 us -> none  [the longest x30 32.6 us: per_device(): jax.scipy.linalg.cho_solve((factor, True), jnp.eye(point_count, dtype=jnp...]
    psum x1 -> x0, blocking collectives: 46.7 us -> none  [per_device(): at_points = lax.psum(partial_rows, ('gz', 'gy')).astype(jnp.bfloat16)]
  transfers between devices with their start and end apart: 2 -> 9, of which waited for: 2 -> 5; matrix products, arithmetic and copies ran while one was open for 0% -> 5% of each run, Pallas kernels for 0% -> 24%
where the time goes in v1:
time: 349 us; the launch traced here: 348 us
  Pallas kernels  148 us (42%)
  blocking collectives  77.7 us (22%)
  waiting for transfers between devices  31.8 us (9%)
  local copies, waits for them, and re-layouts  29.7 us (9%)
  other arithmetic  22.6 us (6%)
  starting transfers between devices  17.4 us (5%)
  between operations  13.6 us (4%)
  matrix products  6.95 us (2%)
    all_gather x1, blocking collectives, per_device(): gathered = lax.all_gather(local_values, ('gz', 'gy'), axis=0, tiled=True)  77.7 us
    pallas_call x1, Pallas kernels, invert_gram(): pl.pallas_call(functools.partial(inverse_kernel, big=big, small=small), o...  64.7 us
    pallas_call x1, Pallas kernels, convolve(): pl.pallas_call(column_kernel, grid=(cols // step,), out_shape=(shape, sha...  34.7 us
    pallas_call x1, Pallas kernels, fit(): pl.pallas_call(fit_kernel, grid=(rows // step,), out_shape=jax.ShapeDtype...  29.9 us
    ppermute x7, waiting for transfers between devices, per_device(): part = lax.ppermute(part, ('gz', 'gy'), perm)  24.6 us
    pallas_call x1, Pallas kernels, take_points(): pl.pallas_call(functools.partial(points_kernel, columns=columns), out_sha...  18.6 us
    unnamed x24, local copies, waits for them, and re-layouts  15.5 us
    ppermute x7, starting transfers between devices, per_device(): part = lax.ppermute(part, ('gz', 'gy'), perm)  11.5 us
  transfers between devices with their start and end apart: 9, of which 5 were waited for; matrix products, arithmetic and copies ran while one was open for 5% of the time, Pallas kernels for 24%

profile of v1, /device:TPU:1, one launch (start us, length us, event | category | flops | bytes accessed | tf_op | source)
XLA Modules:
  0.0 347.7 jit_solution(5611097436014720195)
XLA Ops:
  6.5 3.4 copy.14
  10.0 0.1 dynamic-slice_bitcast_fusion
  10.1 0.1 collective-permute-start
  10.2 2.7 collective-permute-start.1
  13.0 1.5 collective-permute-start.2
  14.5 0.8 collective-permute-start.3
  15.3 1.9 collective-permute-start.4
  17.2 0.7 bitcast_dynamic-update-slice_fusion
  17.9 2.0 collective-permute-start.5
  19.9 0.7 constant_dynamic-update-slice_fusion.6
  20.6 1.0 collective-permute-done.1
  21.6 2.4 collective-permute-start.6
  24.0 0.8 constant_dynamic-update-slice_fusion.5
  24.8 2.8 collective-permute-done.2
  27.6 0.7 constant_dynamic-update-slice_fusion.4
  28.3 16.0 %collective-permute-done.3 = bf16[64,8,256]{2,1,0:T(8,128)(2,1)S(1)} collective-permute-done((bf16[64,8,256]{2,1,0:T(8,128)(2,1)S(1)}, bf16[64,8,256]{2,1,0:T(8,128)(2,1)S(1)}, u32[]{:S(2)}, u32[]{:S(2)}) %collective-permute-start.3) | collective-permute-done | bytes 262176 | tf_op jit(solution)/shard_map/ppermute | solution.py:280
  44.3 0.8 constant_dynamic-update-slice_fusion.3
  45.1 4.9 %collective-permute-done.4 = bf16[64,8,256]{2,1,0:T(8,128)(2,1)S(1)} collective-permute-done((bf16[64,8,256]{2,1,0:T(8,128)(2,1)S(1)}, bf16[64,8,256]{2,1,0:T(8,128)(2,1)S(1)}, u32[]{:S(2)}, u32[]{:S(2)}) %collective-permute-start.4) | collective-permute-done | bytes 262176 | tf_op jit(solution)/shard_map/ppermute | solution.py:280
  49.9 0.8 constant_dynamic-update-slice_fusion.2
  50.7 0.7 constant_dynamic-update-slice_fusion.1
  51.4 0.7 constant_dynamic-update-slice_fusion
  52.2 0.1 multiply_add_fusion
  52.3 0.1 add.190
  52.4 0.1 add.187
  52.5 0.1 dynamic-slice_bitcast_fusion.7
  52.6 0.1 copy.15
  52.7 0.3 bitcast_convert_fusion.field_ref
  53.1 18.6 %take_points.1 = f32[8,1024]{1,0:T(8,128)S(1)} custom-call(s32[1024]{0:T(1024)S(1)} %copy-done.3, f32[512,8,256]{2,1,0:T(8,128)S(1)} %bitcast_convert_fusion.field_ref), custom_call_target="tpu_custom_call" | custom-call | tf_op jit(solution)/shard_map/take_points/pallas_call | solution.py:50
  71.7 0.1 broadcast_in_dim.19
  71.7 0.1 broadcast_in_dim.20
  71.9 77.7 %all_gather.11.values_ref = bf16[256,1024]{1,0:T(8,128)(2,1)S(1)} all-gather(bf16[8,1024]{1,0:T(8,128)(2,1)S(1)} %convert_element_type.8), channel_id=1, replica_groups=mesh['gz'=8,'gy'=4] {'gz','gy'}, dimensions={0}, use_global_device_ids=true | all-gather | bytes 540672 | tf_op jit(solution)/shard_map/all_gather | solution.py:263
  149.6 0.6 gather_fusion
  150.2 0.9 constant_dynamic-slice_fusion.2
  151.1 7.0 %reduce-precision_convert_fusion = (bf16[64,64,256]{2,1,0:T(8,128)(2,1)S(1)}, bf16[64,64,256]{2,1,0:T(8,128)(2,1)S(1)}) fusion(f32[512,256,1]{1,0,2:T(8,128)S(1)} %copy-done.7, f32[64,512]{1,0:T(8,128)S(1)} %constant_dynamic-slice_fusion.2, f32[64,512]{1,0:T(8,128)S(1)} %copy.15), kind=kOutput, calls=%fused_computation.5 | convolution fusion | flops 6448742400 | bytes 4980736 | tf_op jit(solution)/shard_map/dot_general | solution.py:306
  158.1 2.5 pad_maximum_fusion.circ_ref
  160.6 0.1 bitcast_select_fusion.2.values_ref
  160.7 64.7 %invert_gram.1 = (bf16[1024,1024]{1,0:T(8,128)(2,1)S(1)}, bf16[1024,1024]{1,0:T(8,128)(2,1)S(1)}) custom-call(bf16[256,1024]{1,0:T(8,128)(2,1)S(1)} %all_gather.11.values_ref), custom_call_target="tpu_custom_call" | custom-call | flops 12884901888 | bytes 6291456 | tf_op jit(solution)/shard_map/invert_gram/pallas_call | solution.py:161
  225.4 1.4 copy-done.5
  226.8 2.2 copy-done.2
  229.0 34.7 %convolve.1 = (bf16[64,64,1024]{2,1,0:T(8,128)(2,1)S(1)}, bf16[64,64,1024]{2,1,0:T(8,128)(2,1)}) custom-call(bf16[4,64,64,256]{3,2,1,0:T(8,128)(2,1)} %bitcast.46, bf16[256,1024]{1,0:T(8,128)(2,1)S(1)} %bitcast_select_fusion.2.values_ref, bf16[64,128,256]{2,1,0:T(8,128)(2,1)S(1)} %copy-done.2), custom_call_target="tpu_custom_call" | custom-call | flops 17179869184 | bytes 25165824 | tf_op jit(solution)/shard_map/convolve/pallas_call | solution.py:201
  263.8 3.3 copy-done.4
  267.0 29.9 %fit.1 = bf16[4096,1024]{1,0:T(8,128)(2,1)} custom-call(bf16[4096,1024]{1,0:T(8,128)(2,1)} %bitcast.42, bf16[4096,1024]{1,0:T(8,128)(2,1)} %bitcast.47, bf16[1024,1024]{1,0:T(8,128)(2,1)S(1)} %get-tuple-element.11.high_ref, bf16[1024,1024]{1,0:T(8,128)(2,1)S(1)} %copy-done.6), custom_call_target="tpu_custom_call" | custom-call | flops 25769803776 | bytes 29360128 | tf_op jit(solution)/shard_map/fit/pallas_call | solution.py:234
  296.9 7.0 %constant_dynamic-slice_fusion.1 = (bf16[64,1,32,1024]{3,2,1,0:T(8,128)(2,1)}, bf16[64,1,32,1024]{3,2,1,0:T(8,128)(2,1)S(1)}) fusion(bf16[64,2,32,1024]{3,2,1,0:T(8,128)(2,1)} %bitcast.45, s32[]{:T(128)S(6)} %select_n.138, s32[]{:T(128)S(6)} %select_n.155), kind=kLoop, calls=%fused_computation.34 | loop fusion | bytes 16777224 | tf_op jit(solution)/shard_map/jit(dynamic_index_in_dim)/dynamic_slice | solution.py:316
  303.9 4.3 %copy.21 = bf16[64,1,32,1024]{3,0,2,1:T(8,128)(2,1)} copy(bf16[64,1,32,1024]{3,2,1,0:T(8,128)(2,1)S(1)} %get-tuple-element.16) | data formatting | bytes 8388608 | tf_op jit(solution)/shard_map/jit(dynamic_index_in_dim)/dynamic_slice | solution.py:317
  308.2 6.0 %collective-permute-start.7 = (bf16[64,32,1024]{2,0,1:T(8,128)(2,1)}, bf16[64,32,1024]{2,0,1:T(8,128)(2,1)}, u32[]{:S(2)}, u32[]{:S(2)}) collective-permute-start(bf16[64,32,1024]{2,0,1:T(8,128)(2,1)} %bitcast.40), channel_id=1, source_target_pairs={{0,4},{4,0},{8,12},{12,8},{16,20},{20,16},{24,28},{28,24},{1,5},{5... | collective-permute-start | bytes 12582920 | tf_op jit(solution)/shard_map/ppermute | solution.py:318
  314.2 7.1 %collective-permute-done.7 = bf16[64,32,1024]{2,0,1:T(8,128)(2,1)} collective-permute-done((bf16[64,32,1024]{2,0,1:T(8,128)(2,1)}, bf16[64,32,1024]{2,0,1:T(8,128)(2,1)}, u32[]{:S(2)}, u32[]{:S(2)}) %collective-permute-start.7) | collective-permute-done | bytes 4194336 | tf_op jit(solution)/shard_map/ppermute | solution.py:318
  321.3 11.0 %bitcast_select_fusion.1 = (bf16[64,32,1024]{2,0,1:T(8,128)(2,1)}, bf16[64,32,1024]{2,0,1:T(8,128)(2,1)}) fusion(bf16[64,32,1024]{2,0,1:T(8,128)(2,1)} %collective-permute-done.7, pred[]{:T(512)S(6)} %eq.17, bf16[64,1,32,1024]{3,2,1,0:T(8,128)(2,1)} %get-tuple-element.15), kind=kLoop, calls=%fused_computation.9 | loop fusion | flops 4194304 | bytes 16777216 | tf_op jit(solution)/shard_map/jit(_where)/select_n | solution.py:319
  332.3 8.5 %maximum_bitcast_fusion = bf16[32,128,1024]{2,1,0:T(8,128)(2,1)} fusion(bf16[64,32,1024]{2,0,1:T(8,128)(2,1)} %get-tuple-element.14, bf16[64,32,1024]{2,0,1:T(8,128)(2,1)} %get-tuple-element.13), kind=kLoop, calls=%fused_computation.1 | loop fusion | flops 16777216 | bytes 16777216 | tf_op jit(solution)/shard_map/transpose | solution.py:321
  (26 shorter events, 0.1 us)
Async XLA Ops:
  6.5 45.9 %copy-start = (f32[256,128]{1,0:T(8,128)S(1)}, f32[256,128]{1,0:T(8,128)}, u32[]{:S(2)}) copy-start(f32[256,128]{1,0:T(8,128)} %param.7) | copy-start | bytes 393220
  6.5 220.3 %all-gather.3.cloned.1.call-start = ((), (), s32[]{:S(2)}) async-start(), calls=%async_computation | async-start | bytes 10485760 | tf_op jit(solution)/shard_map/all_gather | solution.py:284
  10.1 7.8 %collective-permute-start = (bf16[64,8,256]{2,1,0:T(8,128)(2,1)S(1)}, bf16[64,8,256]{2,1,0:T(8,128)(2,1)S(1)}, u32[]{:S(2)}, u32[]{:S(2)}) collective-permute-start(bf16[64,8,256]{2,1,0:T(8,128)(2,1)S(1)} %get-tuple-element.25), channel_id=1, source_target_pairs={{0,4},{1,5},{2,6},{3,7},{4,0},{5,1},{6,2},{7,3},{8,12},{9,13},{10,... | collective-permute-start | bytes 786440 | tf_op jit(solution)/shard_map/ppermute | solution.py:280
  10.2 11.4 %collective-permute-start.1 = (bf16[64,8,256]{2,1,0:T(8,128)(2,1)S(1)}, bf16[64,8,256]{2,1,0:T(8,128)(2,1)S(1)}, u32[]{:S(2)}, u32[]{:S(2)}) collective-permute-start(bf16[64,8,256]{2,1,0:T(8,128)(2,1)S(1)} %get-tuple-element.24), channel_id=1, source_target_pairs={{0,1},{1,2},{2,3},{3,0},{4,5},{5,6},{6,7},{7,4},{8,9},{9,10},{10,1... | collective-permute-start | bytes 786440 | tf_op jit(solution)/shard_map/ppermute | solution.py:280
  13.0 14.6 %collective-permute-start.2 = (bf16[64,8,256]{2,1,0:T(8,128)(2,1)S(1)}, bf16[64,8,256]{2,1,0:T(8,128)(2,1)S(1)}, u32[]{:S(2)}, u32[]{:S(2)}) collective-permute-start(bf16[64,8,256]{2,1,0:T(8,128)(2,1)S(1)} %get-tuple-element.23), channel_id=1, source_target_pairs={{0,5},{1,6},{2,7},{3,4},{4,1},{5,2},{6,3},{7,0},{8,13},{9,14},{10,... | collective-permute-start | bytes 786440 | tf_op jit(solution)/shard_map/ppermute | solution.py:280
  14.5 29.8 %collective-permute-start.3 = (bf16[64,8,256]{2,1,0:T(8,128)(2,1)S(1)}, bf16[64,8,256]{2,1,0:T(8,128)(2,1)S(1)}, u32[]{:S(2)}, u32[]{:S(2)}) collective-permute-start(bf16[64,8,256]{2,1,0:T(8,128)(2,1)S(1)} %get-tuple-element.22), channel_id=1, source_target_pairs={{0,2},{1,3},{2,0},{3,1},{4,6},{5,7},{6,4},{7,5},{8,10},{9,11},{10,... | collective-permute-start | bytes 786440 | tf_op jit(solution)/shard_map/ppermute | solution.py:280
  15.3 34.6 %collective-permute-start.4 = (bf16[64,8,256]{2,1,0:T(8,128)(2,1)S(1)}, bf16[64,8,256]{2,1,0:T(8,128)(2,1)S(1)}, u32[]{:S(2)}, u32[]{:S(2)}) collective-permute-start(bf16[64,8,256]{2,1,0:T(8,128)(2,1)S(1)} %get-tuple-element.21), channel_id=1, source_target_pairs={{0,6},{1,7},{2,4},{3,5},{4,2},{5,3},{6,0},{7,1},{8,14},{9,15},{10,... | collective-permute-start | bytes 786440 | tf_op jit(solution)/shard_map/ppermute | solution.py:280
  17.9 32.7 %collective-permute-start.5 = (bf16[64,8,256]{2,1,0:T(8,128)(2,1)S(1)}, bf16[64,8,256]{2,1,0:T(8,128)(2,1)S(1)}, u32[]{:S(2)}, u32[]{:S(2)}) collective-permute-start(bf16[64,8,256]{2,1,0:T(8,128)(2,1)S(1)} %get-tuple-element.20), channel_id=1, source_target_pairs={{0,3},{1,0},{2,1},{3,2},{4,7},{5,4},{6,5},{7,6},{8,11},{9,8},{10,9... | collective-permute-start | bytes 786440 | tf_op jit(solution)/shard_map/ppermute | solution.py:280
  21.6 29.8 %collective-permute-start.6 = (bf16[64,8,256]{2,1,0:T(8,128)(2,1)S(1)}, bf16[64,8,256]{2,1,0:T(8,128)(2,1)S(1)}, u32[]{:S(2)}, u32[]{:S(2)}) collective-permute-start(bf16[64,8,256]{2,1,0:T(8,128)(2,1)S(1)} %get-tuple-element.19), channel_id=1, source_target_pairs={{0,7},{1,4},{2,5},{3,6},{4,3},{5,0},{6,1},{7,2},{8,15},{9,12},{10,... | collective-permute-start | bytes 786440 | tf_op jit(solution)/shard_map/ppermute | solution.py:280
  52.2 0.9 copy-start.3
  53.1 98.1 %copy-start.7 = (f32[512,256,1]{1,0,2:T(8,128)S(1)}, f32[512,256,1]{1,0,2:T(8,128)}, u32[]{:S(2)}) copy-start(f32[512,256,1]{1,0,2:T(8,128)} %constant.128) | copy-start | bytes 1572868
  225.4 1.4 copy-start.5
  226.8 2.2 copy-start.2
  229.0 38.0 %copy-start.6 = (bf16[1024,1024]{1,0:T(8,128)(2,1)S(1)}, bf16[1024,1024]{1,0:T(8,128)(2,1)}, u32[]{:S(2)}) copy-start(bf16[1024,1024]{1,0:T(8,128)(2,1)} %copy-done.5) | copy-start | bytes 6291460
  263.8 3.3 copy-start.4
  308.2 13.1 %collective-permute-start.7 = (bf16[64,32,1024]{2,0,1:T(8,128)(2,1)}, bf16[64,32,1024]{2,0,1:T(8,128)(2,1)}, u32[]{:S(2)}, u32[]{:S(2)}) collective-permute-start(bf16[64,32,1024]{2,0,1:T(8,128)(2,1)} %bitcast.40), channel_id=1, source_target_pairs={{0,4},{4,0},{8,12},{12,8},{16,20},{20,16},{24,28},{28,24},{1,5},{5... | collective-permute-start | bytes 12582920 | tf_op jit(solution)/shard_map/ppermute | solution.py:318
  332.3 8.5 %copy-start.1 = (f32[256,128]{1,0:T(8,128)S(1)}, f32[256,128]{1,0:T(8,128)}, u32[]{:S(2)}) copy-start(f32[256,128]{1,0:T(8,128)} %param.7) | copy-start | bytes 393220
Sparse Core Ops, SparseCore 0:
  52.3 99.6 all-gather.2
